TPU v7x, 32 devices: a whole 2x2x4 slice. The times are simulated.
32 devices in a mesh: lev: 8 (over z, x), mem: 4 (over y, core).
Axes of the slice: x: 2, y: 2, z: 4, core: 2. Of those that a mesh axis runs over, the one named last changes fastest.
Arguments:
- control: bfloat16 [8, 5, 128, 1024], P('mem', None, 'lev'), may hold values from -6 to 6
- static_control_vector: bfloat16 [5, 128, 1024], P(None, None, 'lev'), may hold values from -6 to 6
- perturb: bfloat16 [8, 5, 128, 1024], P('mem', None, None, 'lev'), may hold values from -6 to 6
- tiles: bfloat16 [4, 64, 64], replicated, may hold values from -0.375 to 0.375
- block_offset: int32 [16, 4], replicated, may hold values from -8 to 8
- vert: bfloat16 [5, 128, 128], replicated, may hold values from -0.5 to 0.5
- static_vertical_root: bfloat16 [5, 128, 128], replicated, may hold values from -0.5 to 0.5
- obs_index: int32 [32768], P(('lev', 'mem')), may hold values from 0 to 20479
- obs_value: float32 [32768], P(('lev', 'mem')), may hold values from -6 to 6
- obs_sigma: float32 [32768], P(('lev', 'mem')), may hold values from 0.3 to 1
- huber_mask: int32 [32768], P(('lev', 'mem')), may hold values 0 or 1
Outputs:
- control_out: bfloat16 [8, 5, 128, 1024], P('mem', None, 'lev')
- static_out: bfloat16 [5, 128, 1024], P(None, None, 'lev')
Inputs may be any that keep to these rules, and one draw needn't show every extreme that they name: `obs_index`: indices count in the block held by the observation's own device: 5 variables, 128 / 4 levels, 128 columns, in that order. `block_offset`: source blocks wrap around the window.
All inputs are finite; a program needn't handle non-finite values. No bound on the sum of `huber_mask` on one device may be relied on, other than what follows from the above.
Results may differ from a plain program's by a relative error of at most 0.0057.
Values may be sent and summed in bfloat16 or wider, within the bound.
A program may use at most 64 MiB of HBM per device.

v0:
```python
import math

import jax
import jax.numpy as jnp
from jax import lax
from jax.sharding import PartitionSpec as P

ITERS = 2


ENS_W = 0.85
STATIC_WEIGHT = 0.5
TAU = 0.5
HUBER_LOW = 0.3


def selectors(block_offset):
    count = block_offset.shape[0]
    blocks = jnp.arange(count, dtype=jnp.int32)
    source = (blocks[:, None] + block_offset) % count
    return (source.T[:, :, None] == blocks[None, None, :]).astype(jnp.bfloat16)


def horizontal(field, tiles, picks):
    count = picks.shape[1]
    width = tiles.shape[1]
    shaped = field.reshape(field.shape[:-1] + (count, width))
    total = None
    for slot in range(tiles.shape[0]):
        moved = jnp.einsum(
            "bj,...jc->...bc", picks[slot], shaped, preferred_element_type=jnp.float32
        ).astype(jnp.bfloat16)
        term = jnp.einsum("...bc,cd->...bd", moved, tiles[slot], preferred_element_type=jnp.float32)
        total = term if total is None else total + term
    return total.reshape(field.shape).astype(jnp.bfloat16)


def horizontal_adjoint(field, tiles, picks):
    count = picks.shape[1]
    width = tiles.shape[1]
    shaped = field.reshape(field.shape[:-1] + (count, width))
    total = None
    for slot in range(tiles.shape[0]):
        term = jnp.einsum(
            "...bc,dc->...bd", shaped, tiles[slot], preferred_element_type=jnp.float32
        )
        moved = jnp.einsum(
            "bj,...bd->...jd",
            picks[slot].astype(jnp.float32),
            term,
            precision=lax.Precision.HIGHEST,
        )
        total = moved if total is None else total + moved
    return total.reshape(field.shape)


def observe(block, obs_index, obs_value, precision_obs):
    flat = block.reshape(-1)
    seen = flat[obs_index]
    resid = precision_obs * (seen - obs_value)
    return jnp.zeros_like(flat).at[obs_index].add(resid).reshape(block.shape)


def on_device(
    control,
    static_control_vector,
    perturb,
    tiles,
    block_offset,
    vert,
    static_vertical_root,
    obs_index,
    obs_value,
    obs_sigma,
    huber_mask,
):
    picks = selectors(block_offset)
    members_all = control.shape[0] * lax.axis_size("mem")
    ens_gain = ENS_W / math.sqrt(members_all)
    level_rows = static_control_vector.shape[1] // lax.axis_size("mem")
    first_level = lax.axis_index("mem") * level_rows
    weights = jnp.where(huber_mask == 1, jnp.float32(1.0), jnp.float32(HUBER_LOW))
    precision_obs = weights / (obs_sigma * obs_sigma)
    vertical_forward = vert.astype(jnp.float32)
    static_forward = static_vertical_root.astype(jnp.float32)
    for turn in range(ITERS):
        local = horizontal(control, tiles, picks)
        columns = lax.all_to_all(local, "lev", split_axis=3, concat_axis=2, tiled=True)
        vertical = jnp.einsum("vlk,mvkc->mvlc", vert, columns, preferred_element_type=jnp.float32)
        partial_value = jnp.sum(vertical * perturb.astype(jnp.float32), axis=0)
        static_portion = jnp.einsum(
            "tbu,tuo->tbo",
            static_vertical_root,
            static_control_vector,
            preferred_element_type=jnp.float32,
        )
        ens = lax.psum_scatter(partial_value, "mem", scatter_dimension=1, tiled=True)
        own_static = lax.dynamic_slice_in_dim(static_portion, first_level, level_rows, 1)
        increment = ens_gain * ens + STATIC_WEIGHT * own_static
        grad_block = observe(increment, obs_index, obs_value, precision_obs)
        gradient_field_total = lax.all_gather(grad_block, "mem", axis=1, tiled=True)
        static_gradient = static_control_vector.astype(jnp.float32) + STATIC_WEIGHT * jnp.einsum(
            "otn,ote->one", static_forward, gradient_field_total, precision=lax.Precision.HIGHEST
        )
        weighted_innovations = (ens_gain * gradient_field_total)[None] * perturb.astype(jnp.float32)
        backward_field = jnp.einsum(
            "vkl,mvkc->mvlc",
            vertical_forward,
            weighted_innovations,
            precision=lax.Precision.HIGHEST,
        ).astype(jnp.bfloat16)
        levels = lax.all_to_all(backward_field, "lev", split_axis=2, concat_axis=3, tiled=True)
        adjoint = horizontal_adjoint(levels, tiles, picks)
        current = control.astype(jnp.float32)
        control = (current - TAU * (current + adjoint)).astype(jnp.bfloat16)
        static_control_vector = (
            static_control_vector.astype(jnp.float32) - TAU * static_gradient
        ).astype(jnp.bfloat16)
    return (control, static_control_vector)


def solution(mesh):
    placed = (
        P("mem", None, "lev", None),
        P(None, None, "lev"),
        P("mem", None, None, "lev"),
        P(),
        P(),
        P(),
        P(),
        P(("lev", "mem")),
        P(("lev", "mem")),
        P(("lev", "mem")),
        P(("lev", "mem")),
    )
    return jax.shard_map(
        on_device,
        mesh=mesh,
        in_specs=placed,
        out_specs=(P("mem", None, "lev", None), P(None, None, "lev")),
        check_vma=False,
    )
```

profile of v0, /device:TPU:0, one launch (start us, length us, event | category | flops | bytes accessed | tf_op | source)
XLA Modules:
  0.0 216.5 jit_solution(14953253611674242805)
XLA Ops:
  8.0 1.5 reshape.43
  9.5 1.2 fusion.13
  12.3 3.7 %copy.156 = bf16[2,5,16,16,64]{2,0,1,4,3:T(2,128)(2,1)S(1)} copy(bf16[2,5,16,16,64]{4,3,2,1,0:T(8,128)(2,1)S(1)} %fusion.2) | data formatting | bytes 655360 | tf_op jit(solution)/shard_map/convert_element_type | solution.py:35
  16.0 3.4 %reshape.110 = bf16[8,2,10240]{2,1,0:T(2,128)(2,1)} reshape(bf16[1024,5,2,16]{3,2,1,0:T(2,128)(2,1)S(1)} %bitcast.269) | data formatting | bytes 655360
  19.4 7.2 %all-to-all-start = ((bf16[8,2,10240]{2,1,0:T(2,128)(2,1)}), bf16[8,2,10240]{2,1,0:T(2,128)(2,1)S(1)}, u32[]{:S(2)}, u32[]{:S(2)}) async-start(bf16[8,2,10240]{2,1,0:T(2,128)(2,1)} %reshape.110), calls=%async_computation | async-start | bytes 655360 | tf_op jit(solution)/shard_map/all_to_all | solution.py:88
  26.7 1.2 copy.105
  27.9 9.1 %all-to-all-done = bf16[8,2,10240]{2,1,0:T(2,128)(2,1)S(1)} async-done(((bf16[8,2,10240]{2,1,0:T(2,128)(2,1)}), bf16[8,2,10240]{2,1,0:T(2,128)(2,1)S(1)}, u32[]{:S(2)}, u32[]{:S(2)}) %all-to-all-start) | async-done | bytes 327712 | tf_op jit(solution)/shard_map/all_to_all | solution.py:88
  37.0 1.9 reshape.111
  38.8 1.6 copy.172
  42.0 19.4 %reduce-scatter.3.cloned.1.call-done = f32[5,32,128]{2,1,0:T(8,128)} async-done(((f32[5,128,128]{2,1,0:T(8,128)}), f32[5,32,128]{2,1,0:T(8,128)}) %reduce-scatter.3.cloned.1.call-update) | async-done | bytes 81936 | tf_op jit(solution)/shard_map/reduce_scatter | solution.py:97
  61.3 0.9 multiply_add_fusion
  62.3 6.2 %gather_fusion = f32[1024]{0:T(1024)S(1)} fusion(f32[20480]{0:T(1024)S(1)} %bitcast.268, s32[1024]{0:T(1024)S(1)} %get-tuple-element.12), kind=kCustom, calls=%fused_computation | custom fusion | bytes 12288 | tf_op jit(solution)/shard_map/gather | solution.py:59
  68.5 5.9 %scatter_custom_fusion = f32[20480]{0:T(1024)S(1)} fusion(s32[1024]{0:T(1024)S(1)} %get-tuple-element.13, f32[1024]{0:T(1024)S(1)} %subtract_multiply_fusion.1, f32[]{:T(128)} %constant.13.clone.1), kind=kCustom, calls=%fused_computation.80 | custom fusion | flops 1024 | bytes 81924 | tf_op jit(solution)/shard_map/scatter-add | solution.py:61
  74.4 6.0 %all_gather.6 = f32[5,128,128]{2,1,0:T(8,128)S(1)} all-gather(f32[5,32,128]{2,1,0:T(8,128)S(1)} %bitcast.278), channel_id=1, replica_groups=mesh['lev'=8,'mem'=4] {'mem'}, dimensions={1}, use_global_device_ids=true | all-gather | bytes 409600 | tf_op jit(solution)/shard_map/all_gather | solution.py:101
  81.8 16.7 %all_to_all.66 = bf16[2,5,128,128]{3,0,1,2:T(2,128)(2,1)S(1)} all-to-all(bf16[2,5,128,128]{3,0,1,2:T(2,128)(2,1)S(1)} %copy.108), channel_id=1, replica_groups=mesh['lev'=8,'mem'=4] {'lev'}, dimensions={2} | all-to-all | bytes 655360 | tf_op jit(solution)/shard_map/all_to_all | solution.py:112
  105.4 1.6 convolution_add_fusion.5
  107.0 1.8 convolution_add_fusion.4
  108.9 1.4 fusion.3
  110.2 6.4 %copy.164 = bf16[2,5,16,16,64]{2,0,1,4,3:T(2,128)(2,1)S(1)} copy(bf16[2,5,16,16,64]{4,3,2,1,0:T(8,128)(2,1)} %fusion.3) | data formatting | bytes 655360 | tf_op jit(solution)/shard_map/convert_element_type | solution.py:35
  116.6 3.4 %reshape.112 = bf16[8,2,10240]{2,1,0:T(2,128)(2,1)} reshape(bf16[1024,5,2,16]{3,2,1,0:T(2,128)(2,1)S(1)} %bitcast.271) | data formatting | bytes 655360
  120.0 13.9 %all_to_all.67 = bf16[8,2,10240]{2,1,0:T(2,128)(2,1)} all-to-all(bf16[8,2,10240]{2,1,0:T(2,128)(2,1)} %reshape.112), channel_id=1, replica_groups=mesh['lev'=8,'mem'=4] {'lev'}, dimensions={0} | all-to-all | bytes 655360 | tf_op jit(solution)/shard_map/all_to_all | solution.py:88
  133.9 8.5 %reshape.113 = bf16[1024,5,2,16]{3,2,1,0:T(2,128)(2,1)S(1)} reshape(bf16[8,2,10240]{2,1,0:T(2,128)(2,1)} %all_to_all.67) | data formatting | bytes 655360
  142.5 3.5 %copy.173 = bf16[2,5,16,8,128]{4,2,3,0,1:T(8,128)(2,1)} copy(bf16[2,5,16,8,128]{2,0,1,4,3:T(2,128)(2,1)S(1)} %bitcast.272) | data formatting | bytes 655360 | tf_op jit(solution)/shard_map/all_to_all | solution.py:88
  145.9 1.4 fusion.17
  147.3 0.9 copy.119
  149.1 17.3 %reduce-scatter.5.cloned.1.call-done = f32[5,32,128]{2,1,0:T(8,128)} async-done(((f32[5,128,128]{2,1,0:T(8,128)}), f32[5,32,128]{2,1,0:T(8,128)}) %reduce-scatter.5.cloned.1.call-update) | async-done | bytes 81936 | tf_op jit(solution)/shard_map/reduce_scatter | solution.py:97
  167.3 6.2 %gather_fusion.1 = f32[1024]{0:T(1024)S(1)} fusion(f32[20480]{0:T(1024)S(1)} %bitcast.267, s32[1024]{0:T(1024)S(1)} %get-tuple-element.12), kind=kCustom, calls=%fused_computation.1 | custom fusion | bytes 12288 | tf_op jit(solution)/shard_map/gather | solution.py:59
  173.5 5.9 %scatter_custom_fusion.1 = f32[20480]{0:T(1024)S(1)} fusion(s32[1024]{0:T(1024)S(1)} %get-tuple-element.13, f32[1024]{0:T(1024)S(1)} %subtract_multiply_fusion, f32[]{:T(128)} %constant.13.clone.1), kind=kCustom, calls=%fused_computation.78 | custom fusion | flops 1024 | bytes 81924 | tf_op jit(solution)/shard_map/scatter-add | solution.py:61
  179.5 6.0 %all_gather.7 = f32[5,128,128]{2,1,0:T(8,128)S(1)} all-gather(f32[5,32,128]{2,1,0:T(8,128)S(1)} %bitcast.277), channel_id=1, replica_groups=mesh['lev'=8,'mem'=4] {'mem'}, dimensions={1}, use_global_device_ids=true | all-gather | bytes 409600 | tf_op jit(solution)/shard_map/all_gather | solution.py:101
  186.1 1.3 copy.124
  187.3 5.5 %all-to-all-start.3 = ((bf16[2,5,128,128]{3,0,1,2:T(2,128)(2,1)}), bf16[2,5,128,128]{3,0,1,2:T(2,128)(2,1)S(1)}, u32[]{:S(2)}, u32[]{:S(2)}) async-start(bf16[2,5,128,128]{3,0,1,2:T(2,128)(2,1)} %copy.124), calls=%async_computation.5 | async-start | bytes 655360 | tf_op jit(solution)/shard_map/all_to_all | solution.py:112
  194.4 9.3 %all-to-all-done.3 = bf16[2,5,128,128]{3,0,1,2:T(2,128)(2,1)S(1)} async-done(((bf16[2,5,128,128]{3,0,1,2:T(2,128)(2,1)}), bf16[2,5,128,128]{3,0,1,2:T(2,128)(2,1)S(1)}, u32[]{:S(2)}, u32[]{:S(2)}) %all-to-all-start.3) | async-done | bytes 327712 | tf_op jit(solution)/shard_map/all_to_all | solution.py:112
  (85 shorter events, 22.0 us)
Async XLA Ops:
  7.2 33.3 %copy-start = (bf16[5,128,128]{2,1,0:T(8,128)(2,1)S(1)}, bf16[5,128,128]{2,1,0:T(8,128)(2,1)}, u32[]{:S(2)}) copy-start(bf16[5,128,128]{2,1,0:T(8,128)(2,1)} %param.16) | copy-start | bytes 491524
  8.0 2.7 %copy-start.6 = (bf16[4,64,64]{2,1,0:T(8,128)(2,1)S(1)}, bf16[4,64,64]{2,1,0:T(8,128)(2,1)}, u32[]{:S(2)}) copy-start(bf16[4,64,64]{2,1,0:T(8,128)(2,1)} %param.14) | copy-start | bytes 98308
  19.4 17.6 %all-to-all-start = ((bf16[8,2,10240]{2,1,0:T(2,128)(2,1)}), bf16[8,2,10240]{2,1,0:T(2,128)(2,1)S(1)}, u32[]{:S(2)}, u32[]{:S(2)}) async-start(bf16[8,2,10240]{2,1,0:T(2,128)(2,1)} %reshape.110), calls=%async_computation | async-start | bytes 655360 | tf_op jit(solution)/shard_map/all_to_all | solution.py:88
  26.6 34.7 %reduce-scatter.3.cloned.1.call-start = ((), (), s32[]{:S(2)}) async-start(), calls=%async_computation.6 | async-start | bytes 409600 | tf_op jit(solution)/shard_map/reduce_scatter | solution.py:97
  40.4 1.3 copy-start.12
  40.4 1.3 copy-start.3
  40.4 1.3 copy-start.7
  41.7 124.7 %reduce-scatter.5.cloned.1.call-start = ((), (), s32[]{:S(2)}) async-start(), calls=%async_computation.7 | async-start | bytes 409600 | tf_op jit(solution)/shard_map/reduce_scatter | solution.py:97
  62.2 6.2 %copy-start.9 = (f32[1024]{0:T(1024)S(1)}, f32[1024]{0:T(1024)}, u32[]{:S(2)}) copy-start(f32[1024]{0:T(1024)} %param.19) | copy-start | bytes 12292
  62.3 6.2 %copy-start.10 = (f32[1024]{0:T(1024)S(1)}, f32[1024]{0:T(1024)}, u32[]{:S(2)}) copy-start(f32[1024]{0:T(1024)} %param.20) | copy-start | bytes 12292
  62.3 6.2 %copy-start.11 = (s32[1024]{0:T(1024)S(1)}, s32[1024]{0:T(1024)}, u32[]{:S(2)}) copy-start(s32[1024]{0:T(1024)} %param.21) | copy-start | bytes 12292
  80.4 1.4 copy-start.1
  103.4 1.0 copy-start.5
  145.9 2.3 %copy-start.8 = (bf16[5,128,128]{2,1,0:T(8,128)(2,1)S(1)}, bf16[5,128,128]{2,1,0:T(8,128)(2,1)}, u32[]{:S(2)}) copy-start(bf16[5,128,128]{2,1,0:T(8,128)(2,1)} %param.12) | copy-start | bytes 491524
  145.9 2.5 %copy-start.2 = (f32[5,128,128]{2,1,0:T(8,128)S(1)}, f32[5,128,128]{2,1,0:T(8,128)}, u32[]{:S(2)}) copy-start(f32[5,128,128]{2,1,0:T(8,128)} %copy-done.1) | copy-start | bytes 983044
  145.9 2.5 %copy-start.4 = (bf16[5,128,128]{2,1,0:T(8,128)(2,1)S(1)}, bf16[5,128,128]{2,1,0:T(8,128)(2,1)}, u32[]{:S(2)}) copy-start(bf16[5,128,128]{2,1,0:T(8,128)(2,1)} %param.17) | copy-start | bytes 491524
  187.3 16.3 %all-to-all-start.3 = ((bf16[2,5,128,128]{3,0,1,2:T(2,128)(2,1)}), bf16[2,5,128,128]{3,0,1,2:T(2,128)(2,1)S(1)}, u32[]{:S(2)}, u32[]{:S(2)}) async-start(bf16[2,5,128,128]{3,0,1,2:T(2,128)(2,1)} %copy.124), calls=%async_computation.5 | async-start | bytes 655360 | tf_op jit(solution)/shard_map/all_to_all | solution.py:112
Sparse Core Ops, SparseCore 0:
  41.8 19.4 reduce-scatter.2
  148.4 18.0 reduce-scatter.4
where the time goes:
time: 218 us; the launch traced here: 217 us
  local copies, waits for them, and re-layouts  55.4 us (25%)
  waiting for transfers between devices  55 us (25%)
  blocking collectives  42.6 us (20%)
  matrix products  20.6 us (9%)
  other arithmetic  15.5 us (7%)
  between operations  14.6 us (7%)
  starting transfers between devices  12.8 us (6%)
    reduce_scatter x2, waiting for transfers between devices, on_device(): lax.psum_scatter(partial_value, 'mem', scatter_dimension=1, tiled=True)  36.6 us
    unnamed x33, local copies, waits for them, and re-layouts  20 us
    all_to_all x1, blocking collectives, on_device(): lax.all_to_all(backward_field, 'lev', split_axis=2, concat_axis=3, tiled=...  16.7 us
    all_to_all x1, blocking collectives, on_device(): lax.all_to_all(local, 'lev', split_axis=3, concat_axis=2, tiled=True)  13.9 us
    gather x2, local copies, waits for them, and re-layouts, observe(): seen = flat[obs_index]  12.3 us
    all_gather x2, blocking collectives, on_device(): gradient_field_total = lax.all_gather(grad_block, 'mem', axis=1, tiled=True)  11.9 us
    scatter-add x2, other arithmetic, observe(): return jnp.zeros_like(flat).at[obs_index].add(resid).reshape(block.shape)  11.9 us
    convert_element_type x2, local copies, waits for them, and re-layouts, horizontal(): return total.reshape(field.shape).astype(jnp.bfloat16)  10.1 us
  transfers between devices with their start and end apart: 4, of which 4 were waited for; matrix products, arithmetic and copies ran while one was open for 2% of the time, Pallas kernels for 0%

commit v1 on v0

--- a/solution.py
+++ b/solution.py
@@ -1,8 +1,11 @@
+import functools
 import math
 
 import jax
 import jax.numpy as jnp
 from jax import lax
+from jax.experimental import pallas as pl
+from jax.experimental.pallas import tpu as pltpu
 from jax.sharding import PartitionSpec as P
 
 ITERS = 2
@@ -12,6 +15,7 @@
 STATIC_WEIGHT = 0.5
 TAU = 0.5
 HUBER_LOW = 0.3
+MESH = pl.DeviceIdType.MESH
 
 
 def selectors(block_offset):
@@ -119,6 +123,379 @@
     return (control, static_control_vector)
 
 
+def split(value):
+    high = value.astype(jnp.bfloat16)
+    return high, (value - high.astype(jnp.float32)).astype(jnp.bfloat16)
+
+
+def descent_kernel(
+    ens_gain,
+    control_ref,
+    static_ref,
+    perturb_ref,
+    tiles_ref,
+    offset_ref,
+    vert_ref,
+    root_ref,
+    index_ref,
+    value_ref,
+    sigma_ref,
+    mask_ref,
+    control_out,
+    static_out,
+    dense,
+    state,
+    static_state,
+    rows_in,
+    inc0,
+    inc,
+    hot_row,
+    hot_col,
+    fwd_send,
+    fwd_recv,
+    sum_send,
+    sum_recv,
+    grad_recv,
+    bwd_send,
+    bwd_recv,
+    send_sem,
+    recv_sem,
+):
+    members, variables, per_lev, columns = control_ref.shape
+    n_lev = lax.axis_size("lev")
+    n_mem = lax.axis_size("mem")
+    levels = vert_ref.shape[1]
+    per_mem = levels // n_mem
+    width = static_ref.shape[2]
+    block = tiles_ref.shape[1]
+    slots = tiles_ref.shape[0]
+    count = columns // block
+    chunk = members * per_lev
+    my_lev = lax.axis_index("lev")
+    my_mem = lax.axis_index("mem")
+
+    barrier = pltpu.get_barrier_semaphore()
+    for step in range(1, n_lev):
+        pl.semaphore_signal(
+            barrier, inc=1, device_id={"lev": lax.rem(my_lev + step, n_lev)}, device_id_type=MESH
+        )
+    for step in range(1, n_mem):
+        pl.semaphore_signal(
+            barrier, inc=1, device_id={"mem": lax.rem(my_mem + step, n_mem)}, device_id_type=MESH
+        )
+
+    lane = lax.broadcasted_iota(jnp.int32, (1, width), 1)
+    wide = []
+    for slot in range(slots):
+        tile = tiles_ref[slot].astype(jnp.float32)
+        wide.append(jnp.concatenate([tile] * (width // block), axis=1))
+    sources = []
+    for group in range(columns // width):
+        per_slot = []
+        for slot in range(slots):
+            vec = jnp.zeros((1, width), jnp.int32)
+            for part in range(width // block):
+                b = group * (width // block) + part
+                src = lax.rem(lax.rem(b + offset_ref[b, slot], count) + count, count)
+                vec = jnp.where(lane >= part * block, src, vec)
+            per_slot.append(vec)
+        sources.append(per_slot)
+
+    def build(j, carry):
+        for group in range(columns // width):
+            total = jnp.zeros((block, width), jnp.float32)
+            for slot in range(slots):
+                total = total + jnp.where(sources[group][slot] == j, wide[slot], 0.0)
+            dense[pl.ds(pl.multiple_of(j * block, block), block), group * width : (group + 1) * width] = (
+                total.astype(jnp.bfloat16)
+            )
+        return carry
+
+    lax.fori_loop(0, count, build, 0)
+    for v in range(variables):
+        for m in range(members):
+            state[v * chunk + m * per_lev : v * chunk + (m + 1) * per_lev, :] = control_ref[m, v]
+    static_state[...] = static_ref[...]
+    weights = jnp.where(mask_ref[...] == 1, jnp.float32(1.0), jnp.float32(HUBER_LOW))
+    precision_obs = weights / (sigma_ref[...] * sigma_ref[...])
+    pl.semaphore_wait(barrier, n_lev - 1 + n_mem - 1)
+
+    def lev_copy(send, recv, turn, phase, v, peer):
+        return pltpu.make_async_remote_copy(
+            src_ref=send.at[turn, v, peer],
+            dst_ref=recv.at[turn, v, my_lev],
+            send_sem=send_sem.at[turn, phase, v],
+            recv_sem=recv_sem.at[turn, phase, v],
+            device_id={"lev": peer},
+            device_id_type=MESH,
+        )
+
+    def mem_copy(src, dst, turn, phase, v, peer):
+        return pltpu.make_async_remote_copy(
+            src_ref=src,
+            dst_ref=dst,
+            send_sem=send_sem.at[turn, phase, v],
+            recv_sem=recv_sem.at[turn, phase, v],
+            device_id={"mem": peer},
+            device_id_type=MESH,
+        )
+
+    def await_blocks(buffer, sem, turn, phase, v, blocks):
+        part = buffer.at[turn, v, pl.ds(0, blocks)]
+        pltpu.make_async_copy(part, part, sem.at[turn, phase, v]).wait()
+
+    def one_turn(turn, carry):
+        half = 2 * width
+        for pair in range(columns // half):
+            local = jnp.dot(
+                state[...],
+                dense[:, pair * half : (pair + 1) * half],
+                preferred_element_type=jnp.float32,
+            ).astype(jnp.bfloat16)
+            for v in range(variables):
+                for side in range(2):
+                    fwd_send[turn, v, pair * 2 + side] = local[
+                        v * chunk : (v + 1) * chunk, side * width : (side + 1) * width
+                    ]
+        for v in range(variables):
+            for step in range(1, n_lev):
+                lev_copy(fwd_send, fwd_recv, turn, 0, v, lax.rem(my_lev + step, n_lev)).start()
+        for v in range(variables):
+            fwd_recv[turn, v, my_lev] = fwd_send[turn, v, my_lev]
+
+        first = pl.multiple_of(my_mem * per_mem, per_mem)
+        for v in range(variables):
+            inc0[v * per_mem : (v + 1) * per_mem, :] = STATIC_WEIGHT * jnp.dot(
+                root_ref[v, pl.ds(first, per_mem), :],
+                static_state[v],
+                preferred_element_type=jnp.float32,
+            )
+        where_obs = index_ref[...]
+        row_of = where_obs // width
+        col_of = where_obs - row_of * width
+        observations = where_obs.shape[1]
+        hot_row[...] = jnp.where(
+            lax.broadcasted_iota(jnp.int32, (variables * per_mem, observations), 0) == row_of, 1.0, 0.0
+        ).astype(jnp.bfloat16)
+        hot_col[...] = jnp.where(
+            lax.broadcasted_iota(jnp.int32, (width, observations), 0) == col_of, 1.0, 0.0
+        )
+
+        for v in range(variables):
+            await_blocks(fwd_recv, recv_sem, turn, 0, v, n_lev - 1)
+            cols = [
+                fwd_recv[turn, v, :, m * per_lev : (m + 1) * per_lev, :].reshape(levels, width)
+                for m in range(members)
+            ]
+            vertical = jnp.dot(
+                vert_ref[v], jnp.concatenate(cols, axis=1), preferred_element_type=jnp.float32
+            )
+            total = None
+            for m in range(members):
+                term = vertical[:, m * width : (m + 1) * width] * perturb_ref[m, v].astype(jnp.float32)
+                total = term if total is None else total + term
+            sum_send[turn, v] = total.reshape(n_mem, per_mem, width)
+            for step in range(1, n_mem):
+                peer = lax.rem(my_mem + step, n_mem)
+                mem_copy(
+                    sum_send.at[turn, v, peer], sum_recv.at[turn, v, my_mem], turn, 1, v, peer
+                ).start()
+            sum_recv[turn, v, my_mem] = sum_send[turn, v, my_mem]
+        for v in range(variables):
+            await_blocks(sum_recv, recv_sem, turn, 1, v, n_mem - 1)
+            ens = jnp.sum(sum_recv[turn, v], axis=0)
+            own = slice(v * per_mem, (v + 1) * per_mem)
+            inc[own, :] = ens_gain * ens + inc0[own, :]
+
+        high, low = split(inc[...])
+        picked = lax.dot_general(
+            jnp.concatenate([high, low], axis=1),
+            hot_row[...],
+            (((0,), (0,)), ((), ())),
+            preferred_element_type=jnp.float32,
+        )
+        seen = jnp.sum(
+            (picked[:width] + picked[width:]) * hot_col[...], axis=0, keepdims=True
+        )
+        resid = precision_obs * (seen - value_ref[...])
+        high, low = split(hot_col[...] * resid)
+        spread = lax.dot_general(
+            hot_row[...],
+            jnp.concatenate([high, low], axis=0),
+            (((1,), (1,)), ((), ())),
+            preferred_element_type=jnp.float32,
+        )
+        grad = spread[:, :width] + spread[:, width:]
+        for v in range(variables):
+            grad_recv[turn, v, my_mem] = grad[v * per_mem : (v + 1) * per_mem, :]
+            for step in range(1, n_mem):
+                peer = lax.rem(my_mem + step, n_mem)
+                mem_copy(
+                    grad_recv.at[turn, v, my_mem], grad_recv.at[turn, v, my_mem], turn, 2, v, peer
+                ).start()
+
+        for v in range(variables):
+            await_blocks(grad_recv, recv_sem, turn, 2, v, n_mem - 1)
+            field = grad_recv[turn, v].reshape(levels, width)
+            parts = [
+                split((ens_gain * field) * perturb_ref[m, v].astype(jnp.float32))
+                for m in range(members)
+            ]
+            product = lax.dot_general(
+                vert_ref[v],
+                jnp.concatenate([p[0] for p in parts] + [p[1] for p in parts], axis=1),
+                (((0,), (0,)), ((), ())),
+                preferred_element_type=jnp.float32,
+            )
+            back = product[:, : members * width] + product[:, members * width :]
+            for m in range(members):
+                bwd_send[turn, v, :, m * per_lev : (m + 1) * per_lev, :] = (
+                    back[:, m * width : (m + 1) * width]
+                    .astype(jnp.bfloat16)
+                    .reshape(n_lev, per_lev, width)
+                )
+            for step in range(1, n_lev):
+                lev_copy(bwd_send, bwd_recv, turn, 3, v, lax.rem(my_lev + step, n_lev)).start()
+            bwd_recv[turn, v, my_lev] = bwd_send[turn, v, my_lev]
+
+        for v in range(variables):
+            high, low = split(grad_recv[turn, v].reshape(levels, width))
+            product = lax.dot_general(
+                root_ref[v],
+                jnp.concatenate([high, low], axis=1),
+                (((0,), (0,)), ((), ())),
+                preferred_element_type=jnp.float32,
+            )
+            current = static_state[v].astype(jnp.float32)
+            gradient = current + STATIC_WEIGHT * (product[:, :width] + product[:, width:])
+            static_state[v] = (current - TAU * gradient).astype(jnp.bfloat16)
+
+        for v in range(variables):
+            await_blocks(bwd_recv, recv_sem, turn, 3, v, n_lev - 1)
+            for peer in range(n_lev):
+                rows_in[v * chunk : (v + 1) * chunk, peer * width : (peer + 1) * width] = bwd_recv[
+                    turn, v, peer
+                ]
+        for pair in range(columns // half):
+            here = slice(pair * half, (pair + 1) * half)
+            adjoint = lax.dot_general(
+                rows_in[...],
+                dense[here, :],
+                (((1,), (1,)), ((), ())),
+                preferred_element_type=jnp.float32,
+            )
+            current = state[:, here].astype(jnp.float32)
+            state[:, here] = (current - TAU * (current + adjoint)).astype(jnp.bfloat16)
+        return carry
+
+    lax.fori_loop(0, ITERS, one_turn, 0)
+    for v in range(variables):
+        for m in range(members):
+            control_out[m, v] = state[v * chunk + m * per_lev : v * chunk + (m + 1) * per_lev, :]
+    static_out[...] = static_state[...]
+
+    def drain(turn, carry):
+        for v in range(variables):
+            await_blocks(fwd_send, send_sem, turn, 0, v, n_lev - 1)
+            await_blocks(sum_send, send_sem, turn, 1, v, n_mem - 1)
+            await_blocks(grad_recv, send_sem, turn, 2, v, n_mem - 1)
+            await_blocks(bwd_send, send_sem, turn, 3, v, n_lev - 1)
+        return carry
+
+    lax.fori_loop(0, ITERS, drain, 0)
+
+
+def fused(
+    control,
+    static_control_vector,
+    perturb,
+    tiles,
+    block_offset,
+    vert,
+    static_vertical_root,
+    obs_index,
+    obs_value,
+    obs_sigma,
+    huber_mask,
+):
+    members, variables, per_lev, columns = control.shape
+    n_lev, n_mem = lax.axis_size("lev"), lax.axis_size("mem")
+    levels, width = static_control_vector.shape[1:]
+    per_mem = levels // n_mem
+    chunk = members * per_lev
+    observations = obs_index.shape[0]
+    rows = variables * chunk
+    ens_gain = ENS_W / math.sqrt(members * n_mem)
+    vmem = pl.BlockSpec(memory_space=pltpu.VMEM)
+    lev_buffer = pltpu.VMEM((ITERS, variables, n_lev, chunk, width), jnp.bfloat16)
+    mem_buffer = pltpu.VMEM((ITERS, variables, n_mem, per_mem, width), jnp.float32)
+    in_specs = [vmem] * 11
+    in_specs[4] = pl.BlockSpec(memory_space=pltpu.SMEM)
+    flat = (1, observations)
+    return pl.pallas_call(
+        functools.partial(descent_kernel, ens_gain),
+        out_shape=(
+            jax.ShapeDtypeStruct(control.shape, control.dtype),
+            jax.ShapeDtypeStruct(static_control_vector.shape, static_control_vector.dtype),
+        ),
+        in_specs=in_specs,
+        out_specs=(vmem, vmem),
+        scratch_shapes=[
+            pltpu.VMEM((columns, columns), jnp.bfloat16),
+            pltpu.VMEM((rows, columns), jnp.bfloat16),
+            pltpu.VMEM((variables, levels, width), jnp.bfloat16),
+            pltpu.VMEM((rows, columns), jnp.bfloat16),
+            pltpu.VMEM((variables * per_mem, width), jnp.float32),
+            pltpu.VMEM((variables * per_mem, width), jnp.float32),
+            pltpu.VMEM((variables * per_mem, observations), jnp.bfloat16),
+            pltpu.VMEM((width, observations), jnp.float32),
+            lev_buffer,
+            lev_buffer,
+            mem_buffer,
+            mem_buffer,
+            mem_buffer,
+            lev_buffer,
+            lev_buffer,
+            pltpu.SemaphoreType.DMA((ITERS, 4, variables)),
+            pltpu.SemaphoreType.DMA((ITERS, 4, variables)),
+        ],
+        compiler_params=pltpu.CompilerParams(
+            collective_id=0, has_side_effects=True, vmem_limit_bytes=40 * 1024 * 1024
+        ),
+    )(
+        control,
+        static_control_vector,
+        perturb,
+        tiles,
+        block_offset,
+        vert,
+        static_vertical_root,
+        obs_index.reshape(flat),
+        obs_value.reshape(flat),
+        obs_sigma.reshape(flat),
+        huber_mask.reshape(flat),
+    )
+
+
+def suits(control, static_control_vector, tiles):
+    per_lev, columns = control.shape[2:]
+    levels, width = static_control_vector.shape[1:]
+    return (
+        per_lev % 16 == 0
+        and width % 128 == 0
+        and columns % (2 * width) == 0
+        and width % tiles.shape[1] == 0
+        and (levels // lax.axis_size("mem")) % 16 == 0
+        and columns <= 2048
+    )
+
+
+def descent(*arguments):
+    if suits(arguments[0], arguments[1], arguments[3]):
+        return fused(*arguments)
+    return on_device(*arguments)
+
+
 def solution(mesh):
     placed = (
         P("mem", None, "lev", None),
@@ -134,7 +511,7 @@
         P(("lev", "mem")),
     )
     return jax.shard_map(
-        on_device,
+        descent,
         mesh=mesh,
         in_specs=placed,
         out_specs=(P("mem", None, "lev", None), P(None, None, "lev")),

time: 218 us -> 69 us (0.32)
  Pallas kernels: 0 us -> 60.3 us
  waiting for transfers between devices: 55 us -> 0 us
  local copies, waits for them, and re-layouts: 55.4 us -> 7.72 us
  blocking collectives: 42.6 us -> 0 us
  matrix products: 20.6 us -> 0 us
  other arithmetic: 15.5 us -> 0 us
  between operations: 14.6 us -> 0.7 us
  starting transfers between devices: 12.8 us -> 0 us
    pallas_call x0 -> x1, Pallas kernels: none -> 60.3 us  [fused(): pl.pallas_call(functools.partial(descent_kernel, ens_gain), out_shape=(ja...]
    reduce_scatter x2 -> x0, waiting for transfers between devices: 36.6 us -> none  [on_device(): lax.psum_scatter(partial_value, 'mem', scatter_dimension=1, tiled=True)]
    all_to_all x2 -> x0, blocking collectives: 30.7 us -> none  [the longest x1 16.7 us: on_device(): lax.all_to_all(backward_field, 'lev', split_axis=2, concat_axis=3, tiled=...]
    dot_general x32 -> x0, matrix products: 20.6 us -> none  [the longest x8 8.12 us: horizontal(): jnp.einsum('...bc,cd->...bd', moved, tiles[slot], preferred_element_type=...]
    all_to_all x2 -> x0, waiting for transfers between devices: 18.3 us -> none  [the longest x1 9.25 us: on_device(): lax.all_to_all(backward_field, 'lev', split_axis=2, concat_axis=3, tiled=...]
    all_to_all x2 -> x0, starting transfers between devices: 12.8 us -> none  [the longest x1 7.25 us: on_device(): lax.all_to_all(local, 'lev', split_axis=3, concat_axis=2, tiled=True)]
    gather x2 -> x0, local copies, waits for them, and re-layouts: 12.3 us -> none  [observe(): seen = flat[obs_index]]
    unnamed x33 -> x23, local copies, waits for them, and re-layouts: 20 us -> 7.72 us
  transfers between devices with their start and end apart: 4 -> 0, of which waited for: 4 -> 0; matrix products, arithmetic and copies ran while one was open for 2% -> 0% of each run, Pallas kernels for 0% -> 0%
where the time goes in v1:
time: 69 us; the launch traced here: 68.7 us
  Pallas kernels  60.3 us (87%)
  local copies, waits for them, and re-layouts  7.72 us (11%)
  between operations  0.7 us (1%)
    pallas_call x1, Pallas kernels, fused(): pl.pallas_call(functools.partial(descent_kernel, ens_gain), out_shape=(ja...  60.3 us
    unnamed x23, local copies, waits for them, and re-layouts  7.72 us

profile of v1, /device:TPU:0, one launch (start us, length us, event | category | flops | bytes accessed | tf_op | source)
XLA Modules:
  0.0 68.7 jit_solution(17299840401947868050)
XLA Ops:
  0.6 0.0 copy-start.9
  0.6 0.0 copy-start.8
  0.7 0.0 copy-start.6
  0.7 0.0 copy-start.7
  0.7 0.8 %copy.13.offset_ref = s32[16,4]{1,0:T(8,128)S(1)} copy(s32[16,4]{0,1:T(4,128)} %param.15) | data formatting | bytes 512 | tf_op args[4]
  1.5 0.0 copy-done.9
  1.5 0.0 copy-done.8
  1.5 0.0 copy-done.6
  1.5 0.0 copy-done.7
  1.5 0.0 copy-start
  1.5 1.0 %copy-done = bf16[2,5,16,1024]{3,2,1,0:T(8,128)(2,1)S(1)} copy-done((bf16[2,5,16,1024]{3,2,1,0:T(8,128)(2,1)S(1)}, bf16[2,5,16,1024]{3,2,1,0:T(8,128)(2,1)}, u32[]{:S(2)}) %copy-start) | copy-done | bytes 327704
  2.4 0.0 copy-start.1
  2.5 1.0 %copy-done.1 = bf16[2,5,128,128]{3,2,1,0:T(8,128)(2,1)S(1)} copy-done((bf16[2,5,128,128]{3,2,1,0:T(8,128)(2,1)S(1)}, bf16[2,5,128,128]{3,2,1,0:T(8,128)(2,1)}, u32[]{:S(2)}) %copy-start.1) | copy-done | bytes 327704
  3.4 0.0 copy-start.2
  3.4 0.9 %copy-done.2 = bf16[5,128,128]{2,1,0:T(8,128)(2,1)S(1)} copy-done((bf16[5,128,128]{2,1,0:T(8,128)(2,1)S(1)}, bf16[5,128,128]{2,1,0:T(8,128)(2,1)}, u32[]{:S(2)}) %copy-start.2) | copy-done | bytes 163864
  4.3 0.0 copy-start.3
  4.3 0.9 %copy-done.3 = bf16[5,128,128]{2,1,0:T(8,128)(2,1)S(1)} copy-done((bf16[5,128,128]{2,1,0:T(8,128)(2,1)S(1)}, bf16[5,128,128]{2,1,0:T(8,128)(2,1)}, u32[]{:S(2)}) %copy-start.3) | copy-done | bytes 163864
  5.3 0.0 copy-start.4
  5.3 0.9 %copy-done.4 = bf16[5,128,128]{2,1,0:T(8,128)(2,1)S(1)} copy-done((bf16[5,128,128]{2,1,0:T(8,128)(2,1)S(1)}, bf16[5,128,128]{2,1,0:T(8,128)(2,1)}, u32[]{:S(2)}) %copy-start.4) | copy-done | bytes 163864
  6.2 0.0 copy-start.5
  6.2 0.8 %copy-done.5 = bf16[4,64,64]{2,1,0:T(8,128)(2,1)S(1)} copy-done((bf16[4,64,64]{2,1,0:T(8,128)(2,1)S(1)}, bf16[4,64,64]{2,1,0:T(8,128)(2,1)}, u32[]{:S(2)}) %copy-start.5) | copy-done | bytes 32792
  7.0 60.3 %shard_map.122 = (bf16[2,5,16,1024]{3,2,1,0:T(8,128)(2,1)S(1)}, bf16[5,128,128]{2,1,0:T(8,128)(2,1)S(1)}) custom-call(bf16[2,5,16,1024]{3,2,1,0:T(8,128)(2,1)S(1)} %copy-done, bf16[5,128,128]{2,1,0:T(8,128)(2,1)S(1)} %copy-done.2, bf16[2,5,128,128]{3,2,1,0:T(8,128)(2,1)S(1)} %copy-done.1, bf16[4,64,64]{2,1,0:T(8,128)(2,1)S(1)} %copy-done.5, ...), custom_call_target="tpu_custom_call" | custom-call | tf_op jit(solution)/shard_map/pallas_call | solution.py:435
  67.3 0.7 %copy.16 = bf16[2,5,16,1024]{3,2,1,0:T(8,128)(2,1)} copy(bf16[2,5,16,1024]{3,2,1,0:T(8,128)(2,1)S(1)} %get-tuple-element.4) | data formatting | bytes 655360
  68.1 0.7 copy.17
Async XLA Ops:
  0.6 0.8 %copy-start.9 = (s32[1024]{0:T(1024)S(1)}, s32[1024]{0:T(1024)}, u32[]{:S(2)}) copy-start(s32[1024]{0:T(1024)} %param.21) | copy-start | bytes 12292
  0.6 0.8 %copy-start.8 = (f32[1024]{0:T(1024)S(1)}, f32[1024]{0:T(1024)}, u32[]{:S(2)}) copy-start(f32[1024]{0:T(1024)} %param.20) | copy-start | bytes 12292
  0.7 0.8 %copy-start.6 = (s32[1024]{0:T(1024)S(1)}, s32[1024]{0:T(1024)}, u32[]{:S(2)}) copy-start(s32[1024]{0:T(1024)} %param.18) | copy-start | bytes 12292
  0.7 0.8 %copy-start.7 = (f32[1024]{0:T(1024)S(1)}, f32[1024]{0:T(1024)}, u32[]{:S(2)}) copy-start(f32[1024]{0:T(1024)} %param.19) | copy-start | bytes 12292
  1.5 1.0 %copy-start = (bf16[2,5,16,1024]{3,2,1,0:T(8,128)(2,1)S(1)}, bf16[2,5,16,1024]{3,2,1,0:T(8,128)(2,1)}, u32[]{:S(2)}) copy-start(bf16[2,5,16,1024]{3,2,1,0:T(8,128)(2,1)} %control_ref.1) | copy-start | bytes 983044
  2.4 1.0 %copy-start.1 = (bf16[2,5,128,128]{3,2,1,0:T(8,128)(2,1)S(1)}, bf16[2,5,128,128]{3,2,1,0:T(8,128)(2,1)}, u32[]{:S(2)}) copy-start(bf16[2,5,128,128]{3,2,1,0:T(8,128)(2,1)} %perturb_ref.1) | copy-start | bytes 983044
  3.4 0.9 %copy-start.2 = (bf16[5,128,128]{2,1,0:T(8,128)(2,1)S(1)}, bf16[5,128,128]{2,1,0:T(8,128)(2,1)}, u32[]{:S(2)}) copy-start(bf16[5,128,128]{2,1,0:T(8,128)(2,1)} %static_ref.1) | copy-start | bytes 491524
  4.3 0.9 %copy-start.3 = (bf16[5,128,128]{2,1,0:T(8,128)(2,1)S(1)}, bf16[5,128,128]{2,1,0:T(8,128)(2,1)}, u32[]{:S(2)}) copy-start(bf16[5,128,128]{2,1,0:T(8,128)(2,1)} %vert_ref.1) | copy-start | bytes 491524
  5.3 0.9 %copy-start.4 = (bf16[5,128,128]{2,1,0:T(8,128)(2,1)S(1)}, bf16[5,128,128]{2,1,0:T(8,128)(2,1)}, u32[]{:S(2)}) copy-start(bf16[5,128,128]{2,1,0:T(8,128)(2,1)} %root_ref.1) | copy-start | bytes 491524
  6.2 0.8 %copy-start.5 = (bf16[4,64,64]{2,1,0:T(8,128)(2,1)S(1)}, bf16[4,64,64]{2,1,0:T(8,128)(2,1)}, u32[]{:S(2)}) copy-start(bf16[4,64,64]{2,1,0:T(8,128)(2,1)} %tiles_ref.1) | copy-start | bytes 98308

commit v2 on v1

--- a/solution.py
+++ b/solution.py
@@ -130,25 +130,33 @@
 
 def descent_kernel(
     ens_gain,
-    control_ref,
-    static_ref,
+    control_hbm,
+    static_hbm,
+    perturb_hbm,
+    tiles_hbm,
+    offset_ref,
+    vert_hbm,
+    root_hbm,
+    index_hbm,
+    value_hbm,
+    sigma_hbm,
+    mask_hbm,
+    control_out,
+    static_out,
     perturb_ref,
     tiles_ref,
-    offset_ref,
     vert_ref,
     root_ref,
     index_ref,
     value_ref,
     sigma_ref,
     mask_ref,
-    control_out,
-    static_out,
     dense,
     state,
     static_state,
     rows_in,
     inc0,
-    inc,
+    precision_obs,
     hot_row,
     hot_col,
     fwd_send,
@@ -160,13 +168,14 @@
     bwd_recv,
     send_sem,
     recv_sem,
+    fetch_sem,
 ):
-    members, variables, per_lev, columns = control_ref.shape
+    members, variables, per_lev, columns = control_hbm.shape
     n_lev = lax.axis_size("lev")
     n_mem = lax.axis_size("mem")
     levels = vert_ref.shape[1]
     per_mem = levels // n_mem
-    width = static_ref.shape[2]
+    width = static_state.shape[2]
     block = tiles_ref.shape[1]
     slots = tiles_ref.shape[0]
     count = columns // block
@@ -183,6 +192,32 @@
         pl.semaphore_signal(
             barrier, inc=1, device_id={"mem": lax.rem(my_mem + step, n_mem)}, device_id_type=MESH
         )
+
+    tiles_copy = pltpu.make_async_copy(tiles_hbm, tiles_ref, fetch_sem.at[0])
+    tiles_copy.start()
+    for v in range(variables):
+        for m in range(members):
+            pltpu.make_async_copy(
+                control_hbm.at[m, v],
+                state.at[pl.ds(v * chunk + m * per_lev, per_lev)],
+                fetch_sem.at[1],
+            ).start()
+    late = []
+    for place, (source, target) in enumerate(
+        (
+            (root_hbm, root_ref),
+            (static_hbm, static_state),
+            (index_hbm, index_ref),
+            (vert_hbm, vert_ref),
+            (perturb_hbm, perturb_ref),
+            (value_hbm, value_ref),
+            (sigma_hbm, sigma_ref),
+            (mask_hbm, mask_ref),
+        )
+    ):
+        late.append(pltpu.make_async_copy(source, target, fetch_sem.at[2 + place]))
+        late[-1].start()
+    tiles_copy.wait()
 
     lane = lax.broadcasted_iota(jnp.int32, (1, width), 1)
     wide = []
@@ -196,7 +231,7 @@
             vec = jnp.zeros((1, width), jnp.int32)
             for part in range(width // block):
                 b = group * (width // block) + part
-                src = lax.rem(lax.rem(b + offset_ref[b, slot], count) + count, count)
+                src = lax.rem(lax.rem(b + offset_ref[slot, b], count) + count, count)
                 vec = jnp.where(lane >= part * block, src, vec)
             per_slot.append(vec)
         sources.append(per_slot)
@@ -212,12 +247,7 @@
         return carry
 
     lax.fori_loop(0, count, build, 0)
-    for v in range(variables):
-        for m in range(members):
-            state[v * chunk + m * per_lev : v * chunk + (m + 1) * per_lev, :] = control_ref[m, v]
-    static_state[...] = static_ref[...]
-    weights = jnp.where(mask_ref[...] == 1, jnp.float32(1.0), jnp.float32(HUBER_LOW))
-    precision_obs = weights / (sigma_ref[...] * sigma_ref[...])
+    pltpu.make_async_copy(state, state, fetch_sem.at[1]).wait()
     pl.semaphore_wait(barrier, n_lev - 1 + n_mem - 1)
 
     def lev_copy(send, recv, turn, phase, v, peer):
@@ -244,25 +274,30 @@
         part = buffer.at[turn, v, pl.ds(0, blocks)]
         pltpu.make_async_copy(part, part, sem.at[turn, phase, v]).wait()
 
-    def one_turn(turn, carry):
-        half = 2 * width
+    half = 2 * width
+    cut = (variables + 1) // 2
+    groups = [g for g in (range(cut), range(cut, variables)) if len(g)]
+
+    def forward(turn, group):
+        rows = slice(group[0] * chunk, (group[-1] + 1) * chunk)
         for pair in range(columns // half):
             local = jnp.dot(
-                state[...],
+                state[rows, :],
                 dense[:, pair * half : (pair + 1) * half],
                 preferred_element_type=jnp.float32,
             ).astype(jnp.bfloat16)
-            for v in range(variables):
+            for place, v in enumerate(group):
                 for side in range(2):
                     fwd_send[turn, v, pair * 2 + side] = local[
-                        v * chunk : (v + 1) * chunk, side * width : (side + 1) * width
+                        place * chunk : (place + 1) * chunk, side * width : (side + 1) * width
                     ]
-        for v in range(variables):
+        for v in group:
             for step in range(1, n_lev):
                 lev_copy(fwd_send, fwd_recv, turn, 0, v, lax.rem(my_lev + step, n_lev)).start()
-        for v in range(variables):
+        for v in group:
             fwd_recv[turn, v, my_lev] = fwd_send[turn, v, my_lev]
 
+    def static_forward():
         first = pl.multiple_of(my_mem * per_mem, per_mem)
         for v in range(variables):
             inc0[v * per_mem : (v + 1) * per_mem, :] = STATIC_WEIGHT * jnp.dot(
@@ -270,94 +305,79 @@
                 static_state[v],
                 preferred_element_type=jnp.float32,
             )
-        where_obs = index_ref[...]
-        row_of = where_obs // width
-        col_of = where_obs - row_of * width
-        observations = where_obs.shape[1]
-        hot_row[...] = jnp.where(
-            lax.broadcasted_iota(jnp.int32, (variables * per_mem, observations), 0) == row_of, 1.0, 0.0
-        ).astype(jnp.bfloat16)
-        hot_col[...] = jnp.where(
-            lax.broadcasted_iota(jnp.int32, (width, observations), 0) == col_of, 1.0, 0.0
-        )
-
-        for v in range(variables):
-            await_blocks(fwd_recv, recv_sem, turn, 0, v, n_lev - 1)
-            cols = [
-                fwd_recv[turn, v, :, m * per_lev : (m + 1) * per_lev, :].reshape(levels, width)
-                for m in range(members)
-            ]
-            vertical = jnp.dot(
-                vert_ref[v], jnp.concatenate(cols, axis=1), preferred_element_type=jnp.float32
-            )
-            total = None
-            for m in range(members):
-                term = vertical[:, m * width : (m + 1) * width] * perturb_ref[m, v].astype(jnp.float32)
-                total = term if total is None else total + term
-            sum_send[turn, v] = total.reshape(n_mem, per_mem, width)
-            for step in range(1, n_mem):
-                peer = lax.rem(my_mem + step, n_mem)
-                mem_copy(
-                    sum_send.at[turn, v, peer], sum_recv.at[turn, v, my_mem], turn, 1, v, peer
-                ).start()
-            sum_recv[turn, v, my_mem] = sum_send[turn, v, my_mem]
-        for v in range(variables):
-            await_blocks(sum_recv, recv_sem, turn, 1, v, n_mem - 1)
-            ens = jnp.sum(sum_recv[turn, v], axis=0)
-            own = slice(v * per_mem, (v + 1) * per_mem)
-            inc[own, :] = ens_gain * ens + inc0[own, :]
-
-        high, low = split(inc[...])
+
+    def member_sum(turn, v):
+        await_blocks(fwd_recv, recv_sem, turn, 0, v, n_lev - 1)
+        cols = [
+            fwd_recv[turn, v, :, m * per_lev : (m + 1) * per_lev, :].reshape(levels, width)
+            for m in range(members)
+        ]
+        vertical = jnp.dot(
+            vert_ref[v], jnp.concatenate(cols, axis=1), preferred_element_type=jnp.float32
+        )
+        total = None
+        for m in range(members):
+            term = vertical[:, m * width : (m + 1) * width] * perturb_ref[m, v].astype(jnp.float32)
+            total = term if total is None else total + term
+        sum_send[turn, v] = total.reshape(n_mem, per_mem, width)
+        for step in range(1, n_mem):
+            peer = lax.rem(my_mem + step, n_mem)
+            mem_copy(
+                sum_send.at[turn, v, peer], sum_recv.at[turn, v, my_mem], turn, 1, v, peer
+            ).start()
+        sum_recv[turn, v, my_mem] = sum_send[turn, v, my_mem]
+
+    def observe_one(turn, v):
+        await_blocks(sum_recv, recv_sem, turn, 1, v, n_mem - 1)
+        own = slice(v * per_mem, (v + 1) * per_mem)
+        increment = ens_gain * jnp.sum(sum_recv[turn, v], axis=0) + inc0[own, :]
+        high, low = split(increment)
         picked = lax.dot_general(
             jnp.concatenate([high, low], axis=1),
-            hot_row[...],
+            hot_row[own, :],
             (((0,), (0,)), ((), ())),
             preferred_element_type=jnp.float32,
         )
-        seen = jnp.sum(
-            (picked[:width] + picked[width:]) * hot_col[...], axis=0, keepdims=True
-        )
-        resid = precision_obs * (seen - value_ref[...])
+        seen = jnp.sum((picked[:width] + picked[width:]) * hot_col[...], axis=0, keepdims=True)
+        resid = precision_obs[...] * (seen - value_ref[...])
         high, low = split(hot_col[...] * resid)
         spread = lax.dot_general(
-            hot_row[...],
+            hot_row[own, :],
             jnp.concatenate([high, low], axis=0),
             (((1,), (1,)), ((), ())),
             preferred_element_type=jnp.float32,
         )
-        grad = spread[:, :width] + spread[:, width:]
-        for v in range(variables):
-            grad_recv[turn, v, my_mem] = grad[v * per_mem : (v + 1) * per_mem, :]
-            for step in range(1, n_mem):
-                peer = lax.rem(my_mem + step, n_mem)
-                mem_copy(
-                    grad_recv.at[turn, v, my_mem], grad_recv.at[turn, v, my_mem], turn, 2, v, peer
-                ).start()
-
-        for v in range(variables):
-            await_blocks(grad_recv, recv_sem, turn, 2, v, n_mem - 1)
-            field = grad_recv[turn, v].reshape(levels, width)
-            parts = [
-                split((ens_gain * field) * perturb_ref[m, v].astype(jnp.float32))
-                for m in range(members)
-            ]
-            product = lax.dot_general(
-                vert_ref[v],
-                jnp.concatenate([p[0] for p in parts] + [p[1] for p in parts], axis=1),
-                (((0,), (0,)), ((), ())),
-                preferred_element_type=jnp.float32,
+        grad_recv[turn, v, my_mem] = spread[:, :width] + spread[:, width:]
+        for step in range(1, n_mem):
+            peer = lax.rem(my_mem + step, n_mem)
+            mem_copy(
+                grad_recv.at[turn, v, my_mem], grad_recv.at[turn, v, my_mem], turn, 2, v, peer
+            ).start()
+
+    def vertical_adjoint(turn, v):
+        await_blocks(grad_recv, recv_sem, turn, 2, v, n_mem - 1)
+        field = grad_recv[turn, v].reshape(levels, width)
+        parts = [
+            split((ens_gain * field) * perturb_ref[m, v].astype(jnp.float32)) for m in range(members)
+        ]
+        product = lax.dot_general(
+            vert_ref[v],
+            jnp.concatenate([p[0] for p in parts] + [p[1] for p in parts], axis=1),
+            (((0,), (0,)), ((), ())),
+            preferred_element_type=jnp.float32,
+        )
+        back = product[:, : members * width] + product[:, members * width :]
+        for m in range(members):
+            bwd_send[turn, v, :, m * per_lev : (m + 1) * per_lev, :] = (
+                back[:, m * width : (m + 1) * width]
+                .astype(jnp.bfloat16)
+                .reshape(n_lev, per_lev, width)
             )
-            back = product[:, : members * width] + product[:, members * width :]
-            for m in range(members):
-                bwd_send[turn, v, :, m * per_lev : (m + 1) * per_lev, :] = (
-                    back[:, m * width : (m + 1) * width]
-                    .astype(jnp.bfloat16)
-                    .reshape(n_lev, per_lev, width)
-                )
-            for step in range(1, n_lev):
-                lev_copy(bwd_send, bwd_recv, turn, 3, v, lax.rem(my_lev + step, n_lev)).start()
-            bwd_recv[turn, v, my_lev] = bwd_send[turn, v, my_lev]
-
+        for step in range(1, n_lev):
+            lev_copy(bwd_send, bwd_recv, turn, 3, v, lax.rem(my_lev + step, n_lev)).start()
+        bwd_recv[turn, v, my_lev] = bwd_send[turn, v, my_lev]
+
+    def static_update(turn):
         for v in range(variables):
             high, low = split(grad_recv[turn, v].reshape(levels, width))
             product = lax.dot_general(
@@ -370,7 +390,9 @@
             gradient = current + STATIC_WEIGHT * (product[:, :width] + product[:, width:])
             static_state[v] = (current - TAU * gradient).astype(jnp.bfloat16)
 
-        for v in range(variables):
+    def horizontal_update(turn, group):
+        rows = slice(group[0] * chunk, (group[-1] + 1) * chunk)
+        for v in group:
             await_blocks(bwd_recv, recv_sem, turn, 3, v, n_lev - 1)
             for peer in range(n_lev):
                 rows_in[v * chunk : (v + 1) * chunk, peer * width : (peer + 1) * width] = bwd_recv[
@@ -379,16 +401,45 @@
         for pair in range(columns // half):
             here = slice(pair * half, (pair + 1) * half)
             adjoint = lax.dot_general(
-                rows_in[...],
+                rows_in[rows, :],
                 dense[here, :],
                 (((1,), (1,)), ((), ())),
                 preferred_element_type=jnp.float32,
             )
-            current = state[:, here].astype(jnp.float32)
-            state[:, here] = (current - TAU * (current + adjoint)).astype(jnp.bfloat16)
-        return carry
-
-    lax.fori_loop(0, ITERS, one_turn, 0)
+            current = state[rows, here].astype(jnp.float32)
+            state[rows, here] = (current - TAU * (current + adjoint)).astype(jnp.bfloat16)
+
+    for group in groups:
+        forward(0, group)
+    for copy in late:
+        copy.wait()
+    static_forward()
+    where_obs = index_ref[...]
+    row_of = where_obs // width
+    col_of = where_obs - row_of * width
+    hot_row[...] = jnp.where(
+        lax.broadcasted_iota(jnp.int32, hot_row.shape, 0) == row_of, 1.0, 0.0
+    ).astype(jnp.bfloat16)
+    hot_col[...] = jnp.where(lax.broadcasted_iota(jnp.int32, hot_col.shape, 0) == col_of, 1.0, 0.0)
+    weights = jnp.where(mask_ref[...] == 1, jnp.float32(1.0), jnp.float32(HUBER_LOW))
+    precision_obs[...] = weights / (sigma_ref[...] * sigma_ref[...])
+
+    for turn in range(ITERS):
+        for tick in range(variables + 4):
+            if tick < variables:
+                member_sum(turn, tick)
+            if 0 <= tick - 2 < variables:
+                observe_one(turn, tick - 2)
+            if 0 <= tick - 4 < variables:
+                vertical_adjoint(turn, tick - 4)
+        static_update(turn)
+        if turn + 1 < ITERS:
+            static_forward()
+        for group in groups:
+            horizontal_update(turn, group)
+            if turn + 1 < ITERS:
+                forward(turn + 1, group)
+
     for v in range(variables):
         for m in range(members):
             control_out[m, v] = state[v * chunk + m * per_lev : v * chunk + (m + 1) * per_lev, :]
@@ -429,7 +480,7 @@
     vmem = pl.BlockSpec(memory_space=pltpu.VMEM)
     lev_buffer = pltpu.VMEM((ITERS, variables, n_lev, chunk, width), jnp.bfloat16)
     mem_buffer = pltpu.VMEM((ITERS, variables, n_mem, per_mem, width), jnp.float32)
-    in_specs = [vmem] * 11
+    in_specs = [pl.BlockSpec(memory_space=pl.ANY)] * 11
     in_specs[4] = pl.BlockSpec(memory_space=pltpu.SMEM)
     flat = (1, observations)
     return pl.pallas_call(
@@ -441,12 +492,20 @@
         in_specs=in_specs,
         out_specs=(vmem, vmem),
         scratch_shapes=[
+            pltpu.VMEM(perturb.shape, perturb.dtype),
+            pltpu.VMEM(tiles.shape, tiles.dtype),
+            pltpu.VMEM(vert.shape, vert.dtype),
+            pltpu.VMEM(static_vertical_root.shape, static_vertical_root.dtype),
+            pltpu.VMEM(flat, obs_index.dtype),
+            pltpu.VMEM(flat, obs_value.dtype),
+            pltpu.VMEM(flat, obs_sigma.dtype),
+            pltpu.VMEM(flat, huber_mask.dtype),
             pltpu.VMEM((columns, columns), jnp.bfloat16),
             pltpu.VMEM((rows, columns), jnp.bfloat16),
             pltpu.VMEM((variables, levels, width), jnp.bfloat16),
             pltpu.VMEM((rows, columns), jnp.bfloat16),
             pltpu.VMEM((variables * per_mem, width), jnp.float32),
-            pltpu.VMEM((variables * per_mem, width), jnp.float32),
+            pltpu.VMEM(flat, jnp.float32),
             pltpu.VMEM((variables * per_mem, observations), jnp.bfloat16),
             pltpu.VMEM((width, observations), jnp.float32),
             lev_buffer,
@@ -458,16 +517,17 @@
             lev_buffer,
             pltpu.SemaphoreType.DMA((ITERS, 4, variables)),
             pltpu.SemaphoreType.DMA((ITERS, 4, variables)),
+            pltpu.SemaphoreType.DMA((10,)),
         ],
         compiler_params=pltpu.CompilerParams(
-            collective_id=0, has_side_effects=True, vmem_limit_bytes=40 * 1024 * 1024
+            collective_id=0, has_side_effects=True, vmem_limit_bytes=60 * 1024 * 1024
         ),
     )(
         control,
         static_control_vector,
         perturb,
         tiles,
-        block_offset,
+        block_offset.T,
         vert,
         static_vertical_root,
         obs_index.reshape(flat),

time: 69 us -> 55.7 us (0.81)
  Pallas kernels: 60.3 us -> 52.4 us
  local copies, waits for them, and re-layouts: 7.72 us -> 2.43 us
    pallas_call x1, Pallas kernels: 60.3 us -> 52.4 us  [fused(): pl.pallas_call(functools.partial(descent_kernel, ens_gain), out_shape=(ja...]
    unnamed x23 -> x4, local copies, waits for them, and re-layouts: 7.72 us -> 2.43 us
where the time goes in v2:
time: 55.7 us; the launch traced here: 55.5 us
  Pallas kernels  52.4 us (94%)
  local copies, waits for them, and re-layouts  2.43 us (4%)
  between operations  0.65 us (1%)
    pallas_call x1, Pallas kernels, fused(): pl.pallas_call(functools.partial(descent_kernel, ens_gain), out_shape=(ja...  52.4 us
    unnamed x4, local copies, waits for them, and re-layouts  2.43 us

profile of v2, /device:TPU:0, one launch (start us, length us, event | category | flops | bytes accessed | tf_op | source)
XLA Modules:
  0.0 55.5 jit_solution(10074638418811211859)
XLA Ops:
  0.6 52.4 %shard_map.122 = (bf16[2,5,16,1024]{3,2,1,0:T(8,128)(2,1)}, bf16[5,128,128]{2,1,0:T(8,128)(2,1)}) custom-call(bf16[2,5,16,1024]{3,2,1,0:T(8,128)(2,1)} %control_hbm.1, bf16[5,128,128]{2,1,0:T(8,128)(2,1)} %static_hbm.1, bf16[2,5,128,128]{3,2,1,0:T(8,128)(2,1)} %perturb_hbm.1, bf16[4,64,64]{2,1,0:T(8,128)(2,1)} %tiles_hbm.1, s32[4,16]{1,0:T(4,128)} %bitcast.9, ...), custom_call_target="tpu_custom_call" | custom-call | tf_op jit(solution)/shard_map/pallas_call | solution.py:486
  53.1 0.0 copy-start
  53.1 1.8 %copy.15 = bf16[2,5,16,1024]{3,2,1,0:T(8,128)(2,1)} copy(bf16[2,5,16,1024]{3,2,1,0:T(8,128)(2,1)} %get-tuple-element.4) | data formatting | bytes 655360
  54.8 0.0 copy-done
  54.8 0.7 %copy.16 = bf16[5,128,128]{2,1,0:T(8,128)(2,1)} copy(bf16[5,128,128]{2,1,0:T(8,128)(2,1)S(1)} %copy-done) | data formatting | bytes 327680
Async XLA Ops:
  53.1 1.8 %copy-start = (bf16[5,128,128]{2,1,0:T(8,128)(2,1)S(1)}, bf16[5,128,128]{2,1,0:T(8,128)(2,1)}, u32[]{:S(2)}) copy-start(bf16[5,128,128]{2,1,0:T(8,128)(2,1)} %get-tuple-element.5) | copy-start | bytes 491524

commit v3 on v2

--- a/solution.py
+++ b/solution.py
@@ -340,14 +340,13 @@
         )
         seen = jnp.sum((picked[:width] + picked[width:]) * hot_col[...], axis=0, keepdims=True)
         resid = precision_obs[...] * (seen - value_ref[...])
-        high, low = split(hot_col[...] * resid)
         spread = lax.dot_general(
             hot_row[own, :],
-            jnp.concatenate([high, low], axis=0),
+            (hot_col[...] * resid).astype(jnp.bfloat16),
             (((1,), (1,)), ((), ())),
             preferred_element_type=jnp.float32,
         )
-        grad_recv[turn, v, my_mem] = spread[:, :width] + spread[:, width:]
+        grad_recv[turn, v, my_mem] = spread.astype(jnp.bfloat16)
         for step in range(1, n_mem):
             peer = lax.rem(my_mem + step, n_mem)
             mem_copy(
@@ -356,7 +355,7 @@
 
     def vertical_adjoint(turn, v):
         await_blocks(grad_recv, recv_sem, turn, 2, v, n_mem - 1)
-        field = grad_recv[turn, v].reshape(levels, width)
+        field = grad_recv[turn, v].reshape(levels, width).astype(jnp.float32)
         parts = [
             split((ens_gain * field) * perturb_ref[m, v].astype(jnp.float32)) for m in range(members)
         ]
@@ -379,15 +378,14 @@
 
     def static_update(turn):
         for v in range(variables):
-            high, low = split(grad_recv[turn, v].reshape(levels, width))
             product = lax.dot_general(
                 root_ref[v],
-                jnp.concatenate([high, low], axis=1),
+                grad_recv[turn, v].reshape(levels, width),
                 (((0,), (0,)), ((), ())),
                 preferred_element_type=jnp.float32,
             )
             current = static_state[v].astype(jnp.float32)
-            gradient = current + STATIC_WEIGHT * (product[:, :width] + product[:, width:])
+            gradient = current + STATIC_WEIGHT * product
             static_state[v] = (current - TAU * gradient).astype(jnp.bfloat16)
 
     def horizontal_update(turn, group):
@@ -512,7 +510,7 @@
             lev_buffer,
             mem_buffer,
             mem_buffer,
-            mem_buffer,
+            pltpu.VMEM((ITERS, variables, n_mem, per_mem, width), jnp.bfloat16),
             lev_buffer,
             lev_buffer,
             pltpu.SemaphoreType.DMA((ITERS, 4, variables)),

time: 55.7 us -> 54.6 us (0.980)
  Pallas kernels: 52.4 us -> 51.3 us
    pallas_call x1, Pallas kernels: 52.4 us -> 51.3 us  [fused(): pl.pallas_call(functools.partial(descent_kernel, ens_gain), out_shape=(ja...]
where the time goes in v3:
time: 54.6 us; the launch traced here: 54.4 us
  Pallas kernels  51.3 us (94%)
  local copies, waits for them, and re-layouts  2.43 us (4%)
  between operations  0.65 us (1%)
    pallas_call x1, Pallas kernels, fused(): pl.pallas_call(functools.partial(descent_kernel, ens_gain), out_shape=(ja...  51.3 us
    unnamed x4, local copies, waits for them, and re-layouts  2.43 us

profile of v3, /device:TPU:0, one launch (start us, length us, event | category | flops | bytes accessed | tf_op | source)
XLA Modules:
  0.0 54.4 jit_solution(8314440527496604262)
XLA Ops:
  0.6 51.3 %shard_map.122 = (bf16[2,5,16,1024]{3,2,1,0:T(8,128)(2,1)}, bf16[5,128,128]{2,1,0:T(8,128)(2,1)}) custom-call(bf16[2,5,16,1024]{3,2,1,0:T(8,128)(2,1)} %control_hbm.1, bf16[5,128,128]{2,1,0:T(8,128)(2,1)} %static_hbm.1, bf16[2,5,128,128]{3,2,1,0:T(8,128)(2,1)} %perturb_hbm.1, bf16[4,64,64]{2,1,0:T(8,128)(2,1)} %tiles_hbm.1, s32[4,16]{1,0:T(4,128)} %bitcast.9, ...), custom_call_target="tpu_custom_call" | custom-call | tf_op jit(solution)/shard_map/pallas_call | solution.py:484
  52.0 0.0 copy-start
  52.0 1.8 %copy.15 = bf16[2,5,16,1024]{3,2,1,0:T(8,128)(2,1)} copy(bf16[2,5,16,1024]{3,2,1,0:T(8,128)(2,1)} %get-tuple-element.4) | data formatting | bytes 655360
  53.7 0.0 copy-done
  53.7 0.7 %copy.16 = bf16[5,128,128]{2,1,0:T(8,128)(2,1)} copy(bf16[5,128,128]{2,1,0:T(8,128)(2,1)S(1)} %copy-done) | data formatting | bytes 327680
Async XLA Ops:
  52.0 1.8 %copy-start = (bf16[5,128,128]{2,1,0:T(8,128)(2,1)S(1)}, bf16[5,128,128]{2,1,0:T(8,128)(2,1)}, u32[]{:S(2)}) copy-start(bf16[5,128,128]{2,1,0:T(8,128)(2,1)} %get-tuple-element.5) | copy-start | bytes 491524

commit v4 on v3

--- a/solution.py
+++ b/solution.py
@@ -423,13 +423,13 @@
     precision_obs[...] = weights / (sigma_ref[...] * sigma_ref[...])
 
     for turn in range(ITERS):
-        for tick in range(variables + 4):
+        for tick in range(variables + 3):
             if tick < variables:
                 member_sum(turn, tick)
-            if 0 <= tick - 2 < variables:
-                observe_one(turn, tick - 2)
-            if 0 <= tick - 4 < variables:
-                vertical_adjoint(turn, tick - 4)
+            if 0 <= tick - 1 < variables:
+                observe_one(turn, tick - 1)
+            if 0 <= tick - 3 < variables:
+                vertical_adjoint(turn, tick - 3)
         static_update(turn)
         if turn + 1 < ITERS:
             static_forward()

time: 54.6 us -> 57.4 us (1.051)
  Pallas kernels: 51.3 us -> 54.1 us
    pallas_call x1, Pallas kernels: 51.3 us -> 54.1 us  [fused(): pl.pallas_call(functools.partial(descent_kernel, ens_gain), out_shape=(ja...]
where the time goes in v4:
time: 57.4 us; the launch traced here: 57.2 us
  Pallas kernels  54.1 us (94%)
  local copies, waits for them, and re-layouts  2.43 us (4%)
  between operations  0.65 us (1%)
    pallas_call x1, Pallas kernels, fused(): pl.pallas_call(functools.partial(descent_kernel, ens_gain), out_shape=(ja...  54.1 us
    unnamed x4, local copies, waits for them, and re-layouts  2.43 us

profile of v4, /device:TPU:0, one launch (start us, length us, event | category | flops | bytes accessed | tf_op | source)
XLA Modules:
  0.0 57.2 jit_solution(11061953008053359549)
XLA Ops:
  0.6 54.1 %shard_map.122 = (bf16[2,5,16,1024]{3,2,1,0:T(8,128)(2,1)}, bf16[5,128,128]{2,1,0:T(8,128)(2,1)}) custom-call(bf16[2,5,16,1024]{3,2,1,0:T(8,128)(2,1)} %control_hbm.1, bf16[5,128,128]{2,1,0:T(8,128)(2,1)} %static_hbm.1, bf16[2,5,128,128]{3,2,1,0:T(8,128)(2,1)} %perturb_hbm.1, bf16[4,64,64]{2,1,0:T(8,128)(2,1)} %tiles_hbm.1, s32[4,16]{1,0:T(4,128)} %bitcast.9, ...), custom_call_target="tpu_custom_call" | custom-call | tf_op jit(solution)/shard_map/pallas_call | solution.py:484
  54.8 0.0 copy-start
  54.8 1.8 %copy.15 = bf16[2,5,16,1024]{3,2,1,0:T(8,128)(2,1)} copy(bf16[2,5,16,1024]{3,2,1,0:T(8,128)(2,1)} %get-tuple-element.4) | data formatting | bytes 655360
  56.6 0.0 copy-done
  56.6 0.7 %copy.16 = bf16[5,128,128]{2,1,0:T(8,128)(2,1)} copy(bf16[5,128,128]{2,1,0:T(8,128)(2,1)S(1)} %copy-done) | data formatting | bytes 327680
Async XLA Ops:
  54.8 1.8 %copy-start = (bf16[5,128,128]{2,1,0:T(8,128)(2,1)S(1)}, bf16[5,128,128]{2,1,0:T(8,128)(2,1)}, u32[]{:S(2)}) copy-start(bf16[5,128,128]{2,1,0:T(8,128)(2,1)} %get-tuple-element.5) | copy-start | bytes 491524
